TPU v7x, 256 devices: a whole 4x4x8 slice. The times are simulated.
256 devices in a mesh: tile: 32 (over x_lo, z, core), lev: 8 (over x_hi, y).
Axes of the slice: x: 4 (x_hi: 2, x_lo: 2; x = x_hi * 2 + x_lo), y: 4, z: 8, core: 2. Of those that a mesh axis runs over, the one named last changes fastest.
Arguments:
- gradient: float32 [144, 2, 512, 640], P('lev', None, 'tile'), may hold values from -6 to 6
- land_sea: int32 [144, 512, 640], P('lev', 'tile'), may hold values 0 or 1
- roughness: float32 [144, 512, 640], P('lev', 'tile'), may hold values from 0.5 to 1.4
- scale_index: int32 [10, 144], replicated, may hold values from 0 to 7
- scale_table: float32 [8], replicated, may hold values from 0.03 to 0.12
- balance: float32 [144, 144], replicated, may hold values from -0.5 to 0.5
- corr_a: float32 [144, 144], replicated, may hold values from -0.5 to 0.5
- corr_b: float32 [144, 144], replicated, may hold values from -0.5 to 0.5
Outputs:
- control_grad: float32 [144, 2, 512, 640], P('lev', None, 'tile')
All inputs are finite; a program needn't handle non-finite values. No bound on the sum of `land_sea` on one device may be relied on, other than what follows from the above.
Results may differ from a plain program's by a relative error of at most 0.000098.
Values sent between devices are 32-bit elements; how exact they have to be, the bound alone decides.
A program may use at most 128 MiB of HBM per device.

v0:
```python
import jax
import jax.numpy as jnp
from jax import lax
from jax.experimental import pallas as pl
from jax.experimental.pallas import tpu as pltpu
from jax.sharding import PartitionSpec as P

PASSES = 10
NSCALE = 8
LEVELS = 144
OWN = 18
LON = 16
LAT = 640
LANES = 128
COLS = LAT // LANES
HALO = 10
ROWS = LON + 2 * HALO
MESH = pl.DeviceIdType.MESH
PEERS = ((1, 2), (1, 1), (1, 3), (1, 0), (0, 2), (0, 1), (0, 3))
CHUNKS = ((0, 0), (0, 1), (1, 0), (1, 1))
F32 = jnp.float32
BF16 = jnp.bfloat16


def one_hot(column, shape):
    return (lax.broadcasted_iota(jnp.int32, shape, 1) == column).astype(F32)


def rest_column(row, side):
    owner, pair, level, var = row >> 3, (row >> 2) & 1, (row >> 1) & 1, row & 1
    column = var * 256 + OWN * owner + 16 + level
    return jnp.where(pair == side, column, -1)


def out_rows(side):
    shape = (320, 512)
    row = lax.broadcasted_iota(jnp.int32, shape, 0)
    block, var, owner, level = row >> 7, (row >> 6) & 1, (row >> 3) & 7, row & 7
    main = var * 256 + OWN * owner + 8 * block + level
    return one_hot(jnp.where(row < 256, main, rest_column(row - 256, side)), shape)


def in_rows(side):
    shape = (448, 512)
    row = lax.broadcasted_iota(jnp.int32, shape, 0)
    owner, var, level = row >> 5, (row >> 4) & 1, row & 15
    main = var * 256 + OWN * owner + level
    return one_hot(jnp.where(row < 256, main, rest_column((row - 256) & 63, side)), shape)


def exact_nt(a, b):
    return lax.dot_general(
        a, b, (((1,), (1,)), ((), ())), precision=lax.Precision.HIGHEST, preferred_element_type=F32
    )


def split(x):
    high = x.astype(BF16)
    return high, (x - high.astype(F32)).astype(BF16)


def diffuse(fields, coef, rates):
    lane = lax.broadcasted_iota(jnp.int32, (8, LANES), 1)
    first, last = lane == 0, lane == LANES - 1

    def row_of(ref, row):
        return [ref[row, :, j * LANES : (j + 1) * LANES] for j in range(COLS)]

    def weighted(field, row):
        return [c * f for c, f in zip(row_of(coef, row), row_of(field, row))]

    def one_pass(step, _):
        rate = rates[step]

        def update(row, carry):
            scaled = [rate * c for c in row_of(coef, row)]
            ahead = row_of(coef, row + 1)
            result = []
            for field, (before, now) in zip(fields, carry):
                after = [c * f for c, f in zip(ahead, row_of(field, row + 1))]
                up = [pltpu.roll(w, 1, 1) for w in now]
                down = [pltpu.roll(w, LANES - 1, 1) for w in now]
                for j in range(COLS):
                    lower = jnp.where(first, up[j - 1] if j else now[0], up[j])
                    upper = jnp.where(last, down[j + 1] if j < COLS - 1 else now[j], down[j])
                    spread = (before[j] + after[j]) + (lower + upper) - 4.0 * now[j]
                    own = field[row, :, j * LANES : (j + 1) * LANES]
                    field[row, :, j * LANES : (j + 1) * LANES] = own + scaled[j] * spread
                result.append((now, after))
            return result

        def two(k, carry):
            row = step + 1 + 2 * k
            return update(row + 1, update(row, carry))

        start = [(weighted(f, step), weighted(f, step + 1)) for f in fields]
        lax.fori_loop(0, ROWS // 2 - 1 - step, two, start)
        return 0

    lax.fori_loop(0, PASSES, one_pass, 0)


def kernel(
    grad_hbm, sea_hbm, rough_hbm, index_hbm, table_hbm, balance_hbm, corr_a_hbm, corr_b_hbm, out_hbm,
    grad, sea, rough, index, table, balance, corr_a, corr_b,
    send, send_rest, got, got_rest, mix, mix_rest, field, pairs, rest,
    coef, coef_pairs, coef_rest, rates, natural, weights, operand, result,
    load_sem, small_sem, own_sem, store_sem,
    go_send, go_recv, back_send, back_recv, edge_send, edge_recv, coef_send, coef_recv,
):
    tile, me = lax.axis_index("tile"), lax.axis_index("lev")
    half, y = me // 4, me % 4
    peers = [((half + dx) % 2) * 4 + (y + dy) % 4 for dx, dy in PEERS]
    right, left = (tile + 1) % 32, (tile + 31) % 32

    loads = []
    for n, (source, target) in enumerate(((grad_hbm, grad), (sea_hbm, sea), (rough_hbm, rough))):
        for j in range(COLS):
            copy = pltpu.make_async_copy(
                source.at[:, pl.ds(j * LANES, LANES)], target.at[j], load_sem.at[n, j]
            )
            copy.start()
            loads.append(copy)
    small = []
    pairs_in = (
        (index_hbm, index), (table_hbm, table), (balance_hbm, balance),
        (corr_a_hbm, corr_a), (corr_b_hbm, corr_b),
    )
    for n, (source, target) in enumerate(pairs_in):
        copy = pltpu.make_async_copy(source, target, small_sem.at[n])
        copy.start()
        small.append(copy)

    barrier = pltpu.get_barrier_semaphore()
    for q in peers:
        pl.semaphore_signal(barrier, inc=1, device_id={"lev": q}, device_id_type=MESH)
    for t in (left, right):
        pl.semaphore_signal(barrier, inc=1, device_id={"tile": t}, device_id_type=MESH)

    for copy in loads[:COLS]:
        copy.wait()

    def gather(q, _):
        for i in range(2):
            lon = 2 * q + i
            for j in range(COLS):
                lanes = pl.ds(j * LANES, LANES)
                for v in range(2):
                    for t in range(2):
                        send[q, i, pl.ds(v * 16 + t * 8, 8), lanes] = grad[
                            j, pl.ds(256 * t + 16 * v + lon, 8, stride=32), :
                        ]
                send_rest[q, pl.ds(4 * i, 4), lanes] = grad[j, pl.ds(512 + lon, 4, stride=16), :]
        return 0

    lax.fori_loop(0, 8, gather, 0)
    pl.semaphore_wait(barrier, len(PEERS) + 2)

    def to(q, source, target, sems, at):
        return pltpu.make_async_remote_copy(
            source, target, sems[0].at[at], sems[1].at[at], device_id={"lev": q}, device_id_type=MESH
        )

    go = [[], [], []]
    for part in (2, 0, 1):
        for k, q in enumerate(peers):
            if part < 2:
                copy = to(q, send.at[q, part], got.at[part, me], (go_send, go_recv), (part, k))
            else:
                copy = to(q, send_rest.at[q], got_rest.at[me], (go_send, go_recv), (part, k))
            copy.start()
            go[part].append(copy)
    own = [
        pltpu.make_async_copy(send.at[me, 0], got.at[0, me], own_sem.at[0]),
        pltpu.make_async_copy(send.at[me, 1], got.at[1, me], own_sem.at[1]),
        pltpu.make_async_copy(send_rest.at[me], got_rest.at[me], own_sem.at[2]),
    ]
    for copy in own:
        copy.start()

    for copy in loads[COLS:]:
        copy.wait()

    def coefficients(pair, _):
        for i in range(2):
            lon = 2 * pair + i
            for j in range(COLS):
                lanes = pl.ds(j * LANES, LANES)
                for t in range(2):
                    rows = pl.ds(128 * t + lon, 8, stride=16)
                    coef[t, HALO + lon, :, lanes] = sea[j, rows, :].astype(F32) * rough[j, rows, :]
                for level in range(2):
                    rows = pl.ds(256 + 16 * level + lon, 1)
                    value = sea[j, rows, :].astype(F32) * rough[j, rows, :]
                    coef_pairs[HALO // 2 + pair, pl.ds(4 * i + 2 * level, 2), lanes] = jnp.broadcast_to(
                        value, (2, LANES)
                    )
        return 0

    lax.fori_loop(0, 8, coefficients, 0)

    def edges(ref, span, width, sems, at):
        copies = []
        for n, (target, source, landing) in enumerate(
            ((right, span, 0), (left, width, width + span))
        ):
            copy = pltpu.make_async_remote_copy(
                ref.at[pl.ds(source, width)], ref.at[pl.ds(landing, width)],
                sems[0].at[at, n], sems[1].at[at, n],
                device_id={"tile": target}, device_id_type=MESH,
            )
            copy.start()
            copies.append(copy)
        return copies

    coef_sems = (coef_send, coef_recv)
    coef_edges = [edges(coef.at[t], LON, HALO, coef_sems, t) for t in range(2)]
    coef_edges.append(edges(coef_pairs, LON // 2, HALO // 2, coef_sems, 2))

    for copy in small:
        copy.wait()
    picked = jnp.zeros((PASSES, LEVELS), F32)
    for n in range(NSCALE):
        picked = jnp.where(index[...] == n, table[n], picked)
    column = lax.broadcasted_iota(jnp.int32, (8, LEVELS), 1) - OWN * me
    row = lax.broadcasted_iota(jnp.int32, (8, LEVELS), 0)
    for t, level in enumerate((row, row + 8, 16 + ((row >> 1) & 1))):
        for p in range(PASSES):
            chosen = jnp.where(column == level, jnp.broadcast_to(picked[p : p + 1], (8, LEVELS)), 0.0)
            rates[t, p] = jnp.broadcast_to(jnp.sum(chosen, axis=1, keepdims=True), (8, LANES))

    natural[...] = jnp.zeros((512, 512), F32)
    natural[0:LEVELS, 0:LEVELS] = corr_a[...]
    natural[256 : 256 + LEVELS, 0:LEVELS] = jnp.dot(
        balance[...], corr_a[...], precision=lax.Precision.HIGHEST, preferred_element_type=F32
    )
    natural[256 : 256 + LEVELS, 256 : 256 + LEVELS] = corr_b[...]
    for i in range(2):
        half_way = exact_nt(out_rows(i), natural[...])
        full = exact_nt(half_way, in_rows(i))
        high, low = split(full[:, :256])
        weights[i, :, 0:256] = high
        weights[i, :, 256:512] = high
        weights[i, :, 512:768] = low
        tail = full[:, 256:]
        high = tail.astype(BF16).astype(F32)
        at = lax.broadcasted_iota(jnp.int32, (320, 192), 1)
        weights[i, :, 768:960] = jnp.where(at < 128, high, tail - high).astype(BF16)

    def take(i):
        def block(p, _):
            high, low = split(got[i, p])
            rows = pl.multiple_of(p * 32, 32)
            operand[i, pl.ds(rows, 32), :] = high
            operand[i, pl.ds(256 + rows, 32), :] = low
            operand[i, pl.ds(512 + rows, 32), :] = high
            return 0

        lax.fori_loop(0, 8, block, 0)

    own[2].wait()
    for copy in go[2]:
        copy.wait_recv()
    high, low = split(got_rest[...].reshape(64, LAT))
    for i in range(2):
        operand[i, 768:832, :] = high
        operand[i, 832:896, :] = low
        operand[i, 896:960, :] = high
    for i in range(2):
        own[i].wait()
        for copy in go[i]:
            copy.wait_recv()
        take(i)

    back = []
    for t in range(2):
        for i in range(2):
            mixed = jnp.dot(
                weights[i, 128 * t : 128 * (t + 1), :], operand[i], preferred_element_type=F32
            )
            mix[t, :, :, i] = mixed.reshape(2, 8, 8, LAT)
        for v in range(2):
            copies = []
            rows = pl.ds(HALO + 2 * me, 2)
            for k, q in enumerate(peers):
                copy = to(q, mix.at[t, v, q], field.at[t, v, rows], (back_send, back_recv), (2 * t + v, k))
                copy.start()
                copies.append(copy)
            copy = pltpu.make_async_copy(mix.at[t, v, me], field.at[t, v, rows], own_sem.at[3 + 2 * t + v])
            copy.start()
            back.append((copies, copy))
    mixed = jnp.dot(weights[0, 256:320, :], operand[0], preferred_element_type=F32)
    mixed = mixed + jnp.dot(weights[1, 256:320, :], operand[1], preferred_element_type=F32)
    mix_rest[...] = mixed.reshape(8, 8, LAT)
    copies = []
    for k, q in enumerate(peers):
        copy = to(q, mix_rest.at[q], pairs.at[HALO // 2 + me], (back_send, back_recv), (4, k))
        copy.start()
        copies.append(copy)
    copy = pltpu.make_async_copy(mix_rest.at[me], pairs.at[HALO // 2 + me], own_sem.at[7])
    copy.start()
    back.append((copies, copy))

    edge_sems = (edge_send, edge_recv)

    def arrive(n):
        copies, local = back[n]
        local.wait()
        for copy in copies:
            copy.wait_recv()
        if n < 4:
            return edges(field.at[n // 2, n % 2], LON, HALO, edge_sems, n)
        return edges(pairs, LON // 2, HALO // 2, edge_sems, n)

    def settle(copies):
        for copy in copies:
            copy.wait()

    stores = []

    def store(rows, count, at):
        for j in range(COLS):
            copy = pltpu.make_async_copy(
                result.at[j, pl.ds(rows, count)],
                out_hbm.at[pl.ds(rows, count), pl.ds(j * LANES, LANES)],
                store_sem.at[at, j],
            )
            copy.start()
            stores.append(copy)

    def finish(t, v):
        def place(lon, _):
            for j in range(COLS):
                result[j, pl.ds(256 * t + 16 * v + lon, 8, stride=32), :] = field[
                    t, v, HALO + lon, :, j * LANES : (j + 1) * LANES
                ]
            return 0

        lax.fori_loop(0, LON, place, 0)

    def unpack(source, target, masked):
        top = lax.broadcasted_iota(jnp.int32, (8, LANES), 0) < 4

        def one(pair, _):
            for j in range(COLS):
                lanes = slice(j * LANES, (j + 1) * LANES)
                value = source[pair, :, lanes]
                turned = pltpu.roll(value, 4, 0)
                if masked:
                    value, turned = jnp.where(top, value, 0.0), jnp.where(top, turned, 0.0)
                target[2 * pair, :, lanes] = value
                target[2 * pair + 1, :, lanes] = turned
            return 0

        lax.fori_loop(0, ROWS // 2, one, 0)

    moving = [arrive(0), arrive(1)]
    settle(coef_edges[0])
    settle(coef_edges[1])
    settle(coef_edges[2])
    unpack(coef_pairs, coef_rest, True)
    settle(moving[0])
    settle(moving[1])
    diffuse([field.at[0, 0], field.at[0, 1]], coef.at[0], rates.at[0])
    moving.append(arrive(2))
    moving.append(arrive(3))
    moving.append(arrive(4))
    finish(0, 0)
    finish(0, 1)
    store(0, 256, 0)
    settle(moving[2])
    settle(moving[3])
    diffuse([field.at[1, 0], field.at[1, 1]], coef.at[1], rates.at[1])
    finish(1, 0)
    finish(1, 1)
    store(256, 256, 1)
    settle(moving[4])
    unpack(pairs, rest, False)
    diffuse([rest], coef_rest, rates.at[2])

    def place_rest(lon, _):
        for j in range(COLS):
            result[j, pl.ds(512 + lon, 4, stride=16), :] = rest[
                HALO + lon, 0:4, j * LANES : (j + 1) * LANES
            ]
        return 0

    lax.fori_loop(0, LON, place_rest, 0)
    store(512, 64, 2)
    for copies in go:
        for copy in copies:
            copy.wait_send()
    for copies, _ in back:
        for copy in copies:
            copy.wait_send()
    for copy in stores:
        copy.wait()


def on_device(gradient, land_sea, roughness, scale_index, scale_table, balance, corr_a, corr_b):
    hbm = pl.BlockSpec(memory_space=pl.ANY)
    vmem, dma = pltpu.VMEM, pltpu.SemaphoreType.DMA
    out = pl.pallas_call(
        kernel,
        out_shape=jax.ShapeDtypeStruct((OWN * 2 * LON, LAT), F32),
        in_specs=[hbm] * 8,
        out_specs=hbm,
        scratch_shapes=[
            vmem((COLS, OWN * 2 * LON, LANES), F32),
            vmem((COLS, OWN * LON, LANES), jnp.int32),
            vmem((COLS, OWN * LON, LANES), F32),
            vmem((PASSES, LEVELS), jnp.int32),
            pltpu.SMEM((NSCALE,), F32),
            vmem((LEVELS, LEVELS), F32),
            vmem((LEVELS, LEVELS), F32),
            vmem((LEVELS, LEVELS), F32),
            vmem((8, 2, 32, LAT), F32),
            vmem((8, 8, LAT), F32),
            vmem((2, 8, 32, LAT), F32),
            vmem((8, 8, LAT), F32),
            vmem((2, 2, 8, 2, 8, LAT), F32),
            vmem((8, 8, LAT), F32),
            vmem((2, 2, ROWS, 8, LAT), F32),
            vmem((ROWS // 2, 8, LAT), F32),
            vmem((ROWS, 8, LAT), F32),
            vmem((2, ROWS, 8, LAT), F32),
            vmem((ROWS // 2, 8, LAT), F32),
            vmem((ROWS, 8, LAT), F32),
            vmem((3, PASSES, 8, LANES), F32),
            vmem((512, 512), F32),
            vmem((2, 320, 960), BF16),
            vmem((2, 960, LAT), BF16),
            vmem((COLS, OWN * 2 * LON, LANES), F32),
            dma((3, COLS)),
            dma((5,)),
            dma((8,)),
            dma((3, COLS)),
            dma((3, 7)),
            dma((3, 7)),
            dma((5, 7)),
            dma((5, 7)),
            dma((5, 2)),
            dma((5, 2)),
            dma((3, 2)),
            dma((3, 2)),
        ],
        compiler_params=pltpu.CompilerParams(
            collective_id=0, has_side_effects=True, vmem_limit_bytes=56 * 2**20
        ),
    )(
        gradient.reshape(OWN * 2 * LON, LAT),
        land_sea.reshape(OWN * LON, LAT),
        roughness.reshape(OWN * LON, LAT),
        scale_index,
        scale_table,
        balance,
        corr_a,
        corr_b,
    )
    return out.reshape(OWN, 2, LON, LAT)


def solution(mesh):
    return jax.shard_map(
        on_device,
        mesh=mesh,
        in_specs=(
            P("lev", None, "tile", None),
            P("lev", "tile", None),
            P("lev", "tile", None),
            P(),
            P(),
            P(),
            P(),
            P(),
        ),
        out_specs=P("lev", None, "tile", None),
        check_vma=False,
    )
```

profile of v0, /device:TPU:2, one launch (start us, length us, event | category | flops | bytes accessed | tf_op | source)
XLA Modules:
  0.0 103.7 jit_solution(13323409276304416752)
XLA Ops:
  0.0 101.1 %shard_map.82 = f32[576,640]{1,0:T(8,128)} custom-call(f32[576,640]{1,0:T(8,128)} %bitcast.5, s32[288,640]{1,0:T(8,128)} %bitcast.6, f32[288,640]{1,0:T(8,128)} %bitcast.7, s32[10,144]{1,0:T(8,128)} %index_hbm.1, f32[8]{0:T(128)} %table_hbm.1, f32[144,144]{1,0:T(8,128)} %balance_hbm.1, f32[144,144]{1,0:T(8,128)} %corr_a_hbm.1, f32[144,144]{1,0:T(8,128)} %corr_b_hbm.1), custom_call_target="tpu_custom_call" | custom-call | tf_op jit(solution)/shard_map/pallas_call | solution.py:403
  101.1 2.6 %copy.10 = f32[18,2,16,640]{3,2,1,0:T(8,128)} copy(f32[18,2,16,640]{3,2,1,0:T(8,128)} %bitcast.4) | data formatting | bytes 2949120
where the time goes:
time: 104 us
  Pallas kernels  101 us (97%)
  local copies, waits for them, and re-layouts  2.58 us (2%)
    pallas_call x1, Pallas kernels, on_device(): pl.pallas_call(kernel, out_shape=jax.ShapeDtypeStruct((OWN * 2 * LON, LAT...  101 us
    unnamed x1, local copies, waits for them, and re-layouts  2.58 us

commit v1 on v0

--- a/solution.py
+++ b/solution.py
@@ -17,7 +17,6 @@
 ROWS = LON + 2 * HALO
 MESH = pl.DeviceIdType.MESH
 PEERS = ((1, 2), (1, 1), (1, 3), (1, 0), (0, 2), (0, 1), (0, 3))
-CHUNKS = ((0, 0), (0, 1), (1, 0), (1, 1))
 F32 = jnp.float32
 BF16 = jnp.bfloat16
 
@@ -59,52 +58,67 @@
     return high, (x - high.astype(F32)).astype(BF16)
 
 
-def diffuse(fields, coef, rates):
+def permuted(x, order):
+    high = x.astype(BF16)
+    middle, low = split(x - high.astype(F32))
+    return (moved(high, order) + moved(middle, order)) + moved(low, order)
+
+
+def moved(x, order):
+    return jnp.dot(x, order, preferred_element_type=F32)
+
+
+def diffuse(field, coef, rates):
     lane = lax.broadcasted_iota(jnp.int32, (8, LANES), 1)
     first, last = lane == 0, lane == LANES - 1
+    ahead = 3
 
     def row_of(ref, row):
         return [ref[row, :, j * LANES : (j + 1) * LANES] for j in range(COLS)]
 
-    def weighted(field, row):
-        return [c * f for c, f in zip(row_of(coef, row), row_of(field, row))]
-
-    def one_pass(step, _):
+    def ends(w):
+        return (
+            jnp.where(first, w[0], pltpu.roll(w[-1], 1, 1)),
+            jnp.where(last, w[-1], pltpu.roll(w[0], LANES - 1, 1)),
+        )
+
+    for step in range(PASSES):
         rate = rates[step]
-
-        def update(row, carry):
-            scaled = [rate * c for c in row_of(coef, row)]
-            ahead = row_of(coef, row + 1)
-            result = []
-            for field, (before, now) in zip(fields, carry):
-                after = [c * f for c, f in zip(ahead, row_of(field, row + 1))]
-                up = [pltpu.roll(w, 1, 1) for w in now]
-                down = [pltpu.roll(w, LANES - 1, 1) for w in now]
-                for j in range(COLS):
-                    lower = jnp.where(first, up[j - 1] if j else now[0], up[j])
-                    upper = jnp.where(last, down[j + 1] if j < COLS - 1 else now[j], down[j])
-                    spread = (before[j] + after[j]) + (lower + upper) - 4.0 * now[j]
-                    own = field[row, :, j * LANES : (j + 1) * LANES]
-                    field[row, :, j * LANES : (j + 1) * LANES] = own + scaled[j] * spread
-                result.append((now, after))
-            return result
-
-        def two(k, carry):
-            row = step + 1 + 2 * k
-            return update(row + 1, update(row, carry))
-
-        start = [(weighted(f, step), weighted(f, step + 1)) for f in fields]
-        lax.fori_loop(0, ROWS // 2 - 1 - step, two, start)
+        low, high = step + 1, ROWS - 1 - step
+        rows, outer = {low - 1: row_of(field, low - 1)}, {}
+        for row in range(low, low + ahead):
+            rows[row] = row_of(field, row)
+            outer[row] = ends(rows[row])
+        for row in range(low, high):
+            if row + ahead <= high:
+                rows[row + ahead] = row_of(field, row + ahead)
+                outer[row + ahead] = ends(rows[row + ahead])
+            before, now, after = rows[row - 1], rows[row], rows[row + 1]
+            line = [outer[row][0]] + now + [outer[row][1]]
+            for j, c in enumerate(row_of(coef, row)):
+                total = (before[j] + after[j]) + (line[j] + line[j + 2])
+                field[row, :, j * LANES : (j + 1) * LANES] = now[j] + (rate * c) * (total - 4.0 * now[j])
+
+
+def unpack(source, target):
+    top = lax.broadcasted_iota(jnp.int32, (8, LANES), 0) < 4
+
+    def one(pair, _):
+        for j in range(COLS):
+            lanes = slice(j * LANES, (j + 1) * LANES)
+            value = source[pair, :, lanes]
+            target[2 * pair, :, lanes] = jnp.where(top, value, 0.0)
+            target[2 * pair + 1, :, lanes] = jnp.where(top, pltpu.roll(value, 4, 0), 0.0)
         return 0
 
-    lax.fori_loop(0, PASSES, one_pass, 0)
+    lax.fori_loop(0, ROWS // 2, one, 0)
 
 
 def kernel(
     grad_hbm, sea_hbm, rough_hbm, index_hbm, table_hbm, balance_hbm, corr_a_hbm, corr_b_hbm, out_hbm,
     grad, sea, rough, index, table, balance, corr_a, corr_b,
-    send, send_rest, got, got_rest, mix, mix_rest, field, pairs, rest,
-    coef, coef_pairs, coef_rest, rates, natural, weights, operand, result,
+    send, send_rest, got, got_rest, mix, mix_rest, land, land_rest, wave, wave_pairs,
+    coef, coef_pairs, square, square_pairs, rates, natural, weights, operand, order, back_order, result,
     load_sem, small_sem, own_sem, store_sem,
     go_send, go_recv, back_send, back_recv, edge_send, edge_recv, coef_send, coef_recv,
 ):
@@ -178,6 +192,11 @@
     for copy in own:
         copy.start()
 
+    row = lax.broadcasted_iota(jnp.int32, (LAT, LAT), 0)
+    column = lax.broadcasted_iota(jnp.int32, (LAT, LAT), 1)
+    order[...] = (row == COLS * (column & 127) + (column >> 7)).astype(F32).astype(BF16)
+    back_order[...] = (column == COLS * (row & 127) + (row >> 7)).astype(F32).astype(BF16)
+
     for copy in loads[COLS:]:
         copy.wait()
 
@@ -188,34 +207,44 @@
                 lanes = pl.ds(j * LANES, LANES)
                 for t in range(2):
                     rows = pl.ds(128 * t + lon, 8, stride=16)
-                    coef[t, HALO + lon, :, lanes] = sea[j, rows, :].astype(F32) * rough[j, rows, :]
+                    coef[t, lon, :, lanes] = sea[j, rows, :].astype(F32) * rough[j, rows, :]
                 for level in range(2):
                     rows = pl.ds(256 + 16 * level + lon, 1)
                     value = sea[j, rows, :].astype(F32) * rough[j, rows, :]
-                    coef_pairs[HALO // 2 + pair, pl.ds(4 * i + 2 * level, 2), lanes] = jnp.broadcast_to(
+                    coef_pairs[pair, pl.ds(4 * i + 2 * level, 2), lanes] = jnp.broadcast_to(
                         value, (2, LANES)
                     )
         return 0
 
     lax.fori_loop(0, 8, coefficients, 0)
+    for t in range(2):
+        value = permuted(coef[t].reshape(LON * 8, LAT), order[...]).reshape(LON, 8, LAT)
+        coef[t] = value
+        square[t, HALO : HALO + LON] = value * value
+    value = permuted(coef_pairs[...].reshape(64, LAT), order[...]).reshape(8, 8, LAT)
+    coef_pairs[...] = value
+    square_pairs[HALO // 2 : HALO // 2 + 8] = value * value
 
     def edges(ref, span, width, sems, at):
         copies = []
         for n, (target, source, landing) in enumerate(
             ((right, span, 0), (left, width, width + span))
         ):
-            copy = pltpu.make_async_remote_copy(
-                ref.at[pl.ds(source, width)], ref.at[pl.ds(landing, width)],
-                sems[0].at[at, n], sems[1].at[at, n],
-                device_id={"tile": target}, device_id_type=MESH,
+            copies.append(
+                pltpu.make_async_remote_copy(
+                    ref.at[pl.ds(source, width)], ref.at[pl.ds(landing, width)],
+                    sems[0].at[at, n], sems[1].at[at, n],
+                    device_id={"tile": target}, device_id_type=MESH,
+                )
             )
+        return copies
+
+    coef_sems = (coef_send, coef_recv)
+    coef_edges = [edges(square.at[t], LON, HALO, coef_sems, t) for t in range(2)]
+    coef_edges.append(edges(square_pairs, LON // 2, HALO // 2, coef_sems, 2))
+    for copies in coef_edges:
+        for copy in copies:
             copy.start()
-            copies.append(copy)
-        return copies
-
-    coef_sems = (coef_send, coef_recv)
-    coef_edges = [edges(coef.at[t], LON, HALO, coef_sems, t) for t in range(2)]
-    coef_edges.append(edges(coef_pairs, LON // 2, HALO // 2, coef_sems, 2))
 
     for copy in small:
         copy.wait()
@@ -247,154 +276,151 @@
         at = lax.broadcasted_iota(jnp.int32, (320, 192), 1)
         weights[i, :, 768:960] = jnp.where(at < 128, high, tail - high).astype(BF16)
 
-    def take(i):
-        def block(p, _):
-            high, low = split(got[i, p])
-            rows = pl.multiple_of(p * 32, 32)
-            operand[i, pl.ds(rows, 32), :] = high
-            operand[i, pl.ds(256 + rows, 32), :] = low
-            operand[i, pl.ds(512 + rows, 32), :] = high
-            return 0
-
-        lax.fori_loop(0, 8, block, 0)
+    def take(x, places):
+        high, low = split(x)
+        high, low = moved(high, order[...]).astype(BF16), moved(low, order[...]).astype(BF16)
+        count = x.shape[0]
+        for i, start in places:
+            operand[i, start : start + count, :] = high
+            operand[i, start + count : start + 2 * count, :] = low
+            operand[i, start + 2 * count : start + 3 * count, :] = high
 
     own[2].wait()
     for copy in go[2]:
         copy.wait_recv()
-    high, low = split(got_rest[...].reshape(64, LAT))
-    for i in range(2):
-        operand[i, 768:832, :] = high
-        operand[i, 832:896, :] = low
-        operand[i, 896:960, :] = high
+    take(got_rest[...].reshape(64, LAT), ((0, 768), (1, 768)))
     for i in range(2):
         own[i].wait()
         for copy in go[i]:
             copy.wait_recv()
-        take(i)
-
-    back = []
+        take(got[i].reshape(256, LAT), ((i, 0),))
+
+    back_sems = (back_send, back_recv)
+
+    def back(n):
+        if n < 4:
+            source, target = mix.at[n], land.at[n, pl.ds(2 * me, 2)]
+        else:
+            source, target = mix_rest, land_rest.at[me]
+        remote = [to(q, source.at[q], target, back_sems, (n, k)) for k, q in enumerate(peers)]
+        return remote, pltpu.make_async_copy(source.at[me], target, own_sem.at[3 + n])
+
+    def start_back(n):
+        remote, local = back(n)
+        for copy in remote:
+            copy.start()
+        local.start()
+
     for t in range(2):
         for i in range(2):
             mixed = jnp.dot(
                 weights[i, 128 * t : 128 * (t + 1), :], operand[i], preferred_element_type=F32
             )
-            mix[t, :, :, i] = mixed.reshape(2, 8, 8, LAT)
-        for v in range(2):
-            copies = []
-            rows = pl.ds(HALO + 2 * me, 2)
-            for k, q in enumerate(peers):
-                copy = to(q, mix.at[t, v, q], field.at[t, v, rows], (back_send, back_recv), (2 * t + v, k))
-                copy.start()
-                copies.append(copy)
-            copy = pltpu.make_async_copy(mix.at[t, v, me], field.at[t, v, rows], own_sem.at[3 + 2 * t + v])
-            copy.start()
-            back.append((copies, copy))
+            mix[2 * t : 2 * t + 2, :, i] = mixed.reshape(2, 8, 8, LAT)
+        start_back(2 * t)
+        start_back(2 * t + 1)
     mixed = jnp.dot(weights[0, 256:320, :], operand[0], preferred_element_type=F32)
     mixed = mixed + jnp.dot(weights[1, 256:320, :], operand[1], preferred_element_type=F32)
     mix_rest[...] = mixed.reshape(8, 8, LAT)
-    copies = []
-    for k, q in enumerate(peers):
-        copy = to(q, mix_rest.at[q], pairs.at[HALO // 2 + me], (back_send, back_recv), (4, k))
-        copy.start()
-        copies.append(copy)
-    copy = pltpu.make_async_copy(mix_rest.at[me], pairs.at[HALO // 2 + me], own_sem.at[7])
-    copy.start()
-    back.append((copies, copy))
+    start_back(4)
 
     edge_sems = (edge_send, edge_recv)
 
+    def sides(n):
+        if n < 4:
+            return edges(wave.at[n], LON, HALO, edge_sems, n)
+        return edges(wave_pairs, LON // 2, HALO // 2, edge_sems, n)
+
     def arrive(n):
-        copies, local = back[n]
+        remote, local = back(n)
         local.wait()
-        for copy in copies:
+        for copy in remote:
             copy.wait_recv()
         if n < 4:
-            return edges(field.at[n // 2, n % 2], LON, HALO, edge_sems, n)
-        return edges(pairs, LON // 2, HALO // 2, edge_sems, n)
-
-    def settle(copies):
-        for copy in copies:
-            copy.wait()
-
-    stores = []
+            wave[n, HALO : HALO + LON] = land[n] * coef[n // 2]
+        else:
+            wave_pairs[HALO // 2 : HALO // 2 + 8] = land_rest[...] * coef_pairs[...]
+        for copy in sides(n):
+            copy.start()
 
     def store(rows, count, at):
-        for j in range(COLS):
-            copy = pltpu.make_async_copy(
+        return [
+            pltpu.make_async_copy(
                 result.at[j, pl.ds(rows, count)],
                 out_hbm.at[pl.ds(rows, count), pl.ds(j * LANES, LANES)],
                 store_sem.at[at, j],
             )
-            copy.start()
-            stores.append(copy)
-
-    def finish(t, v):
-        def place(lon, _):
-            for j in range(COLS):
-                result[j, pl.ds(256 * t + 16 * v + lon, 8, stride=32), :] = field[
-                    t, v, HALO + lon, :, j * LANES : (j + 1) * LANES
-                ]
-            return 0
-
-        lax.fori_loop(0, LON, place, 0)
-
-    def unpack(source, target, masked):
-        top = lax.broadcasted_iota(jnp.int32, (8, LANES), 0) < 4
-
-        def one(pair, _):
-            for j in range(COLS):
-                lanes = slice(j * LANES, (j + 1) * LANES)
-                value = source[pair, :, lanes]
-                turned = pltpu.roll(value, 4, 0)
-                if masked:
-                    value, turned = jnp.where(top, value, 0.0), jnp.where(top, turned, 0.0)
-                target[2 * pair, :, lanes] = value
-                target[2 * pair + 1, :, lanes] = turned
-            return 0
-
-        lax.fori_loop(0, ROWS // 2, one, 0)
-
-    moving = [arrive(0), arrive(1)]
-    settle(coef_edges[0])
-    settle(coef_edges[1])
-    settle(coef_edges[2])
-    unpack(coef_pairs, coef_rest, True)
-    settle(moving[0])
-    settle(moving[1])
-    diffuse([field.at[0, 0], field.at[0, 1]], coef.at[0], rates.at[0])
-    moving.append(arrive(2))
-    moving.append(arrive(3))
-    moving.append(arrive(4))
-    finish(0, 0)
-    finish(0, 1)
-    store(0, 256, 0)
-    settle(moving[2])
-    settle(moving[3])
-    diffuse([field.at[1, 0], field.at[1, 1]], coef.at[1], rates.at[1])
-    finish(1, 0)
-    finish(1, 1)
-    store(256, 256, 1)
-    settle(moving[4])
-    unpack(pairs, rest, False)
-    diffuse([rest], coef_rest, rates.at[2])
-
-    def place_rest(lon, _):
+            for j in range(COLS)
+        ]
+
+    def unweighted(value, c, mixed, count):
+        value = jnp.where(c == 0.0, mixed, value / jnp.where(c == 0.0, 1.0, c)).reshape(count, LAT)
+        high, low = split(value)
+        return moved(high, back_order[...]) + moved(low, back_order[...])
+
+    arrive(0)
+    for copies in coef_edges:
+        for copy in copies:
+            copy.wait()
+    unpack(square_pairs, square.at[2])
+
+    def plane(n, _):
+        for k in range(5):
+
+            @pl.when(n == k)
+            def _():
+                if k < 4:
+                    arrive(k + 1)
+                for copy in sides(k):
+                    copy.wait()
+                if k == 4:
+                    unpack(wave_pairs, wave.at[4])
+
+        diffuse(wave.at[n], square.at[n // 2], rates.at[n // 2])
+
+        @pl.when(n < 4)
+        def _():
+            t, v = n // 2, n % 2
+            value = unweighted(wave[n, HALO : HALO + LON], coef[t], land[n], LON * 8)
+            for lon in range(LON):
+                for j in range(COLS):
+                    result[j, pl.ds(256 * t + 16 * v + lon, 8, stride=32), :] = value[
+                        8 * lon : 8 * lon + 8, j * LANES : (j + 1) * LANES
+                    ]
+
+        for t in range(2):
+
+            @pl.when(n == 2 * t + 1)
+            def _():
+                for copy in store(256 * t, 256, t):
+                    copy.start()
+
+        return 0
+
+    lax.fori_loop(0, 5, plane, 0)
+
+    top = lax.broadcasted_iota(jnp.int32, (8, LAT), 0) < 4
+    packed = [
+        jnp.where(top, wave[4, HALO + 2 * p], pltpu.roll(wave[4, HALO + 2 * p + 1], 4, 0))[None]
+        for p in range(8)
+    ]
+    value = unweighted(jnp.concatenate(packed, 0), coef_pairs[...], land_rest[...], 64)
+    for lon in range(LON):
         for j in range(COLS):
-            result[j, pl.ds(512 + lon, 4, stride=16), :] = rest[
-                HALO + lon, 0:4, j * LANES : (j + 1) * LANES
+            result[j, pl.ds(512 + lon, 4, stride=16), :] = value[
+                4 * lon : 4 * lon + 4, j * LANES : (j + 1) * LANES
             ]
-        return 0
-
-    lax.fori_loop(0, LON, place_rest, 0)
-    store(512, 64, 2)
+    for copy in store(512, 64, 2):
+        copy.start()
     for copies in go:
         for copy in copies:
             copy.wait_send()
-    for copies, _ in back:
-        for copy in copies:
+    for n in range(5):
+        for copy in back(n)[0]:
             copy.wait_send()
-    for copy in stores:
-        copy.wait()
+    for at, (rows, count) in enumerate(((0, 256), (256, 256), (512, 64))):
+        for copy in store(rows, count, at):
+            copy.wait()
 
 
 def on_device(gradient, land_sea, roughness, scale_index, scale_table, balance, corr_a, corr_b):
@@ -418,18 +444,22 @@
             vmem((8, 8, LAT), F32),
             vmem((2, 8, 32, LAT), F32),
             vmem((8, 8, LAT), F32),
-            vmem((2, 2, 8, 2, 8, LAT), F32),
+            vmem((4, 8, 2, 8, LAT), F32),
             vmem((8, 8, LAT), F32),
-            vmem((2, 2, ROWS, 8, LAT), F32),
+            vmem((4, LON, 8, LAT), F32),
+            vmem((8, 8, LAT), F32),
+            vmem((5, ROWS, 8, LAT), F32),
             vmem((ROWS // 2, 8, LAT), F32),
-            vmem((ROWS, 8, LAT), F32),
-            vmem((2, ROWS, 8, LAT), F32),
+            vmem((2, LON, 8, LAT), F32),
+            vmem((8, 8, LAT), F32),
+            vmem((3, ROWS, 8, LAT), F32),
             vmem((ROWS // 2, 8, LAT), F32),
-            vmem((ROWS, 8, LAT), F32),
             vmem((3, PASSES, 8, LANES), F32),
             vmem((512, 512), F32),
             vmem((2, 320, 960), BF16),
             vmem((2, 960, LAT), BF16),
+            vmem((LAT, LAT), BF16),
+            vmem((LAT, LAT), BF16),
             vmem((COLS, OWN * 2 * LON, LANES), F32),
             dma((3, COLS)),
             dma((5,)),

time: 104 us -> 71.4 us (0.69)
  Pallas kernels: 101 us -> 68.7 us
    pallas_call x1, Pallas kernels: 101 us -> 68.7 us  [on_device(): pl.pallas_call(kernel, out_shape=jax.ShapeDtypeStruct((OWN * 2 * LON, LAT...]
where the time goes in v1:
time: 71.4 us; the launch traced here: 71.3 us
  Pallas kernels  68.7 us (96%)
  local copies, waits for them, and re-layouts  2.58 us (4%)
    pallas_call x1, Pallas kernels, on_device(): pl.pallas_call(kernel, out_shape=jax.ShapeDtypeStruct((OWN * 2 * LON, LAT...  68.7 us
    unnamed x1, local copies, waits for them, and re-layouts  2.58 us

profile of v1, /device:TPU:2, one launch (start us, length us, event | category | flops | bytes accessed | tf_op | source)
XLA Modules:
  0.0 71.3 jit_solution(4154093060381772713)
XLA Ops:
  0.0 68.7 %shard_map.82 = f32[576,640]{1,0:T(8,128)} custom-call(f32[576,640]{1,0:T(8,128)} %bitcast.5, s32[288,640]{1,0:T(8,128)} %bitcast.6, f32[288,640]{1,0:T(8,128)} %bitcast.7, s32[10,144]{1,0:T(8,128)} %index_hbm.1, f32[8]{0:T(128)} %table_hbm.1, f32[144,144]{1,0:T(8,128)} %balance_hbm.1, f32[144,144]{1,0:T(8,128)} %corr_a_hbm.1, f32[144,144]{1,0:T(8,128)} %corr_b_hbm.1), custom_call_target="tpu_custom_call" | custom-call | tf_op jit(solution)/shard_map/pallas_call | solution.py:429
  68.7 2.6 %copy.10 = f32[18,2,16,640]{3,2,1,0:T(8,128)} copy(f32[18,2,16,640]{3,2,1,0:T(8,128)} %bitcast.4) | data formatting | bytes 2949120

commit v2 on v1

--- a/solution.py
+++ b/solution.py
@@ -17,6 +17,9 @@
 ROWS = LON + 2 * HALO
 MESH = pl.DeviceIdType.MESH
 PEERS = ((1, 2), (1, 1), (1, 3), (1, 0), (0, 2), (0, 1), (0, 3))
+STOPS = (1, 2)
+FIELD_STOPS = (1, 2, 0, 0, 0)
+COEF_STOPS = (1, 2, 0)
 F32 = jnp.float32
 BF16 = jnp.bfloat16
 
@@ -119,8 +122,9 @@
     grad, sea, rough, index, table, balance, corr_a, corr_b,
     send, send_rest, got, got_rest, mix, mix_rest, land, land_rest, wave, wave_pairs,
     coef, coef_pairs, square, square_pairs, rates, natural, weights, operand, order, back_order, result,
+    stop, stop_coef,
     load_sem, small_sem, own_sem, store_sem,
-    go_send, go_recv, back_send, back_recv, edge_send, edge_recv, coef_send, coef_recv,
+    go_send, go_recv, back_send, back_recv, edge_send, edge_recv, coef_send, coef_recv, stop_send, stop_recv,
 ):
     tile, me = lax.axis_index("tile"), lax.axis_index("lev")
     half, y = me // 4, me % 4
@@ -151,6 +155,28 @@
     for t in (left, right):
         pl.semaphore_signal(barrier, inc=1, device_id={"tile": t}, device_id_type=MESH)
 
+    place = tile % 16
+
+    def around(steps):
+        return (tile + steps + 48) % 32
+
+    def stops(d):
+        return ((place == 15, place == 15 - 2 * d, 1), (place == 0, place == 2 * d, -1))
+
+    def greet(t):
+        pl.semaphore_signal(barrier, inc=1, device_id={"tile": t}, device_id_type=MESH)
+
+    for d in STOPS:
+        for at_seam, at_stop, way in stops(d):
+
+            @pl.when(at_stop)
+            def _():
+                greet(around(2 * d * way))
+
+            @pl.when(at_seam)
+            def _():
+                greet(around((2 * d + 1) * way))
+
     for copy in loads[:COLS]:
         copy.wait()
 
@@ -168,7 +194,24 @@
         return 0
 
     lax.fori_loop(0, 8, gather, 0)
-    pl.semaphore_wait(barrier, len(PEERS) + 2)
+    seam, stop_here = False, False
+    for at_seam, _, _ in stops(0):
+        seam = jnp.logical_or(seam, at_seam)
+    for d in STOPS:
+        for _, at_stop, _ in stops(d):
+            stop_here = jnp.logical_or(stop_here, at_stop)
+
+    @pl.when(seam)
+    def _():
+        pl.semaphore_wait(barrier, len(PEERS) + 2 + len(STOPS))
+
+    @pl.when(stop_here)
+    def _():
+        pl.semaphore_wait(barrier, len(PEERS) + 3)
+
+    @pl.when(jnp.logical_not(jnp.logical_or(seam, stop_here)))
+    def _():
+        pl.semaphore_wait(barrier, len(PEERS) + 2)
 
     def to(q, source, target, sems, at):
         return pltpu.make_async_remote_copy(
@@ -239,12 +282,66 @@
             )
         return copies
 
+    def launch(ref, span, width, sems, at, d, kind, buffer):
+        copies = edges(ref, span, width, sems, at)
+        if d == 0:
+            for copy in copies:
+                copy.start()
+            return
+        for n, (at_seam, _, way) in enumerate(stops(d)):
+
+            @pl.when(jnp.logical_not(at_seam))
+            def _():
+                copies[n].start()
+
+            @pl.when(at_seam)
+            def _():
+                pltpu.make_async_remote_copy(
+                    ref.at[pl.ds((span, width)[n], width)], buffer.at[pl.ds(0, width)],
+                    sems[0].at[at, n], stop_recv.at[kind],
+                    device_id={"tile": around(-2 * d * way)}, device_id_type=MESH,
+                ).start()
+
+    def onward(ref, span, width, sems, at, d, kind, buffer):
+        return [
+            (
+                at_stop,
+                pltpu.make_async_remote_copy(
+                    buffer.at[pl.ds(0, width)], buffer.at[pl.ds(0, width)],
+                    stop_send.at[kind], stop_recv.at[kind],
+                    device_id={"tile": around((2 * d + 1) * way)}, device_id_type=MESH,
+                ),
+                pltpu.make_async_remote_copy(
+                    buffer.at[pl.ds(0, width)], ref.at[pl.ds((0, width + span)[n], width)],
+                    stop_send.at[kind], sems[1].at[at, n],
+                    device_id={"tile": around((2 * d + 1) * way)}, device_id_type=MESH,
+                ),
+            )
+            for n, (_, at_stop, way) in enumerate(stops(d))
+        ]
+
+    def pass_on(item):
+        for at_stop, taken, copy in onward(*item):
+
+            @pl.when(at_stop)
+            def _():
+                taken.wait_recv()
+                copy.start()
+
+    def passed_on(item):
+        for at_stop, _, copy in onward(*item):
+
+            @pl.when(at_stop)
+            def _():
+                copy.wait_send()
+
     coef_sems = (coef_send, coef_recv)
-    coef_edges = [edges(square.at[t], LON, HALO, coef_sems, t) for t in range(2)]
-    coef_edges.append(edges(square_pairs, LON // 2, HALO // 2, coef_sems, 2))
-    for copies in coef_edges:
-        for copy in copies:
-            copy.start()
+    coef_items = [
+        (square.at[t], LON, HALO, coef_sems, t, COEF_STOPS[t], 0, stop_coef) for t in range(2)
+    ]
+    coef_items.append((square_pairs, LON // 2, HALO // 2, coef_sems, 2, COEF_STOPS[2], 0, stop_coef))
+    for item in coef_items:
+        launch(*item)
 
     for copy in small:
         copy.wait()
@@ -276,6 +373,10 @@
         at = lax.broadcasted_iota(jnp.int32, (320, 192), 1)
         weights[i, :, 768:960] = jnp.where(at < 128, high, tail - high).astype(BF16)
 
+    for n in range(3):
+        if COEF_STOPS[n]:
+            pass_on(coef_items[n])
+
     def take(x, places):
         high, low = split(x)
         high, low = moved(high, order[...]).astype(BF16), moved(low, order[...]).astype(BF16)
@@ -326,10 +427,10 @@
 
     edge_sems = (edge_send, edge_recv)
 
-    def sides(n):
+    def side_item(n):
         if n < 4:
-            return edges(wave.at[n], LON, HALO, edge_sems, n)
-        return edges(wave_pairs, LON // 2, HALO // 2, edge_sems, n)
+            return (wave.at[n], LON, HALO, edge_sems, n, FIELD_STOPS[n], 1, stop)
+        return (wave_pairs, LON // 2, HALO // 2, edge_sems, n, FIELD_STOPS[n], 1, stop)
 
     def arrive(n):
         remote, local = back(n)
@@ -340,8 +441,9 @@
             wave[n, HALO : HALO + LON] = land[n] * coef[n // 2]
         else:
             wave_pairs[HALO // 2 : HALO // 2 + 8] = land_rest[...] * coef_pairs[...]
-        for copy in sides(n):
-            copy.start()
+        launch(*side_item(n))
+        if FIELD_STOPS[n]:
+            pass_on(side_item(n))
 
     def store(rows, count, at):
         return [
@@ -359,8 +461,9 @@
         return moved(high, back_order[...]) + moved(low, back_order[...])
 
     arrive(0)
-    for copies in coef_edges:
-        for copy in copies:
+    arrive(1)
+    for item in coef_items:
+        for copy in edges(*item[:5]):
             copy.wait()
     unpack(square_pairs, square.at[2])
 
@@ -369,9 +472,9 @@
 
             @pl.when(n == k)
             def _():
-                if k < 4:
-                    arrive(k + 1)
-                for copy in sides(k):
+                if k < 3:
+                    arrive(k + 2)
+                for copy in edges(*side_item(k)[:5]):
                     copy.wait()
                 if k == 4:
                     unpack(wave_pairs, wave.at[4])
@@ -418,6 +521,12 @@
     for n in range(5):
         for copy in back(n)[0]:
             copy.wait_send()
+    for n in range(3):
+        if COEF_STOPS[n]:
+            passed_on(coef_items[n])
+    for n in range(5):
+        if FIELD_STOPS[n]:
+            passed_on(side_item(n))
     for at, (rows, count) in enumerate(((0, 256), (256, 256), (512, 64))):
         for copy in store(rows, count, at):
             copy.wait()
@@ -461,6 +570,8 @@
             vmem((LAT, LAT), BF16),
             vmem((LAT, LAT), BF16),
             vmem((COLS, OWN * 2 * LON, LANES), F32),
+            vmem((HALO, 8, LAT), F32),
+            vmem((HALO, 8, LAT), F32),
             dma((3, COLS)),
             dma((5,)),
             dma((8,)),
@@ -473,6 +584,8 @@
             dma((5, 2)),
             dma((3, 2)),
             dma((3, 2)),
+            dma((2,)),
+            dma((2,)),
         ],
         compiler_params=pltpu.CompilerParams(
             collective_id=0, has_side_effects=True, vmem_limit_bytes=56 * 2**20

time: 71.4 us -> 63.2 us (0.89)
  Pallas kernels: 68.7 us -> 59.8 us
    pallas_call x1, Pallas kernels: 68.7 us -> 59.8 us  [on_device(): pl.pallas_call(kernel, out_shape=jax.ShapeDtypeStruct((OWN * 2 * LON, LAT...]
where the time goes in v2:
time: 63.2 us; the launch traced here: 62.4 us
  Pallas kernels  59.8 us (95%)
  local copies, waits for them, and re-layouts  2.58 us (4%)
    pallas_call x1, Pallas kernels, on_device(): pl.pallas_call(kernel, out_shape=jax.ShapeDtypeStruct((OWN * 2 * LON, LAT...  59.8 us
    unnamed x1, local copies, waits for them, and re-layouts  2.58 us

profile of v2, /device:TPU:2, one launch (start us, length us, event | category | flops | bytes accessed | tf_op | source)
XLA Modules:
  0.0 62.4 jit_solution(5164700699989841437)
XLA Ops:
  0.0 59.8 %shard_map.82 = f32[576,640]{1,0:T(8,128)} custom-call(f32[576,640]{1,0:T(8,128)} %bitcast.5, s32[288,640]{1,0:T(8,128)} %bitcast.6, f32[288,640]{1,0:T(8,128)} %bitcast.7, s32[10,144]{1,0:T(8,128)} %index_hbm.1, f32[8]{0:T(128)} %table_hbm.1, f32[144,144]{1,0:T(8,128)} %balance_hbm.1, f32[144,144]{1,0:T(8,128)} %corr_a_hbm.1, f32[144,144]{1,0:T(8,128)} %corr_b_hbm.1), custom_call_target="tpu_custom_call" | custom-call | tf_op jit(solution)/shard_map/pallas_call | solution.py:538
  59.8 2.6 %copy.10 = f32[18,2,16,640]{3,2,1,0:T(8,128)} copy(f32[18,2,16,640]{3,2,1,0:T(8,128)} %bitcast.4) | data formatting | bytes 2949120
